TPU v7x, 256 devices: a whole 4x4x8 slice. The times are simulated.
256 devices in a mesh: dp: 64 (over z, x_hi, y), tensor: 4 (over x_lo, core).
Axes of the slice: x: 4 (x_hi: 2, x_lo: 2; x = x_hi * 2 + x_lo), y: 4, z: 8, core: 2. Of those that a mesh axis runs over, the one named last changes fastest.
Arguments:
- cotangent: bfloat16 [32768, 4608], P(('dp', 'tensor')), may hold values from -24 to 24
- attn_saved: bfloat16 [32768, 2048], P('dp', 'tensor'), may hold values from -6 to 6
- attn_next: bfloat16 [32768, 2048], P('dp', 'tensor'), may hold values from -6 to 6
- weight: bfloat16 [4608, 2048], P('dp', 'tensor'), may hold values from -0.125 to 0.125
- moment1: float32 [4608, 2048], P('dp', 'tensor'), may hold values from -6 to 6
- moment2: float32 [4608, 2048], P('dp', 'tensor'), may hold values from 0.1 to 10
Outputs:
- grad_attn: bfloat16 [32768, 2048], P('dp', 'tensor')
- new_weight: bfloat16 [4608, 2048], P('dp', 'tensor')
- new_moment1: float32 [4608, 2048], P('dp', 'tensor')
- new_moment2: float32 [4608, 2048], P('dp', 'tensor')
- next_out: bfloat16 [32768, 4608], P(('dp', 'tensor'))
All inputs are finite; a program needn't handle non-finite values.
Results may differ from a plain program's by a relative error of at most 0.013.
Values may be sent and summed in bfloat16 or wider, within the bound.
A program may use at most 128 MiB of HBM per device.

v0:
```python
import math

import jax
import jax.numpy as jnp
from jax import lax
from jax.sharding import PartitionSpec as P

first_decay = 0.9
second_decay = 0.95
first_fix = 1.0 - 0.9**10
second_fix = 1.0 - 0.95**10
learning_rate = 0.002
weight_decay = 0.1
epsilon = 1e-08


def adamw_step(gradient, weight, moment1, moment2):
    new_moment1 = first_decay * moment1 + (1.0 - first_decay) * gradient
    new_moment2 = second_decay * moment2 + (1.0 - second_decay) * gradient * gradient
    update = new_moment1 / first_fix / (jnp.sqrt(new_moment2 / second_fix) + epsilon)
    new_weight = (
        weight.astype(jnp.float32) * (1.0 - learning_rate * weight_decay) - learning_rate * update
    ).astype(jnp.bfloat16)
    return (new_weight, new_moment1, new_moment2)


def local(cotangent, attn_saved, attn_next, weight, moment1, moment2):
    gathered = lax.all_gather(cotangent, "tensor", axis=0, tiled=True)
    tok_rows = gathered.shape[0]
    scale = 1.0 / math.sqrt(tok_rows * lax.axis_size("dp"))
    columns = gathered
    grad_attn = jnp.dot(
        columns,
        lax.all_gather(weight, "dp", axis=0, tiled=True),
        preferred_element_type=jnp.float32,
    ).astype(jnp.bfloat16)
    columns = gathered
    product = lax.dot_general(
        columns, attn_saved, (((0,), (0,)), ((), ())), preferred_element_type=jnp.float32
    )
    gradient = lax.psum_scatter(product * scale, "dp", scatter_dimension=0, tiled=True)
    new_weight, new_moment1, new_moment2 = adamw_step(gradient, weight, moment1, moment2)
    partial_out = lax.dot_general(
        attn_next,
        lax.all_gather(new_weight, "dp", axis=0, tiled=True),
        (((1,), (1,)), ((), ())),
        preferred_element_type=jnp.float32,
    )
    next_out = lax.psum_scatter(
        partial_out.astype(jnp.bfloat16), "tensor", scatter_dimension=0, tiled=True
    )
    return (grad_attn, new_weight, new_moment1, new_moment2, next_out)


def solution(mesh):
    return jax.shard_map(
        local,
        mesh=mesh,
        in_specs=(
            P(("dp", "tensor"), None),
            P("dp", "tensor"),
            P("dp", "tensor"),
            P("dp", "tensor"),
            P("dp", "tensor"),
            P("dp", "tensor"),
        ),
        out_specs=(
            P("dp", "tensor"),
            P("dp", "tensor"),
            P("dp", "tensor"),
            P("dp", "tensor"),
            P(("dp", "tensor"), None),
        ),
        check_vma=False,
    )
```

profile of v0, /device:TPU:1, one launch (start us, length us, event | category | flops | bytes accessed | tf_op | source)
XLA Modules:
  0.0 1220.9 jit_solution(2917888469098331701)
XLA Ops:
  7.2 0.0 copy-start
  7.2 0.0 all-gather.4.cloned.1.call-start
  7.2 0.7 all-gather.4.cloned.1.call-update
  7.9 0.0 reduce-scatter.5.cloned.1.call-start
  8.0 59.6 %all-gather.4.cloned.1.call-done = bf16[512,4608]{1,0:T(8,128)(2,1)} async-done(((bf16[128,4608]{1,0:T(8,128)(2,1)}), bf16[512,4608]{1,0:T(8,128)(2,1)}) %all-gather.4.cloned.1.call-update) | async-done | bytes 4718608 | tf_op jit(solution)/shard_map/all_gather | solution.py:28
  67.5 0.0 copy-done
  67.5 7.5 convolution_multiply_fusion
  75.1 0.0 reduce-scatter.5.cloned.1.call-update
  75.1 0.0 all-gather.8.cloned.1.call-start
  75.1 819.2 %reduce-scatter.5.cloned.1.call-done = f32[72,512]{1,0:T(8,128)} async-done(((f32[4608,512]{1,0:T(8,128)}), f32[72,512]{1,0:T(8,128)}) %reduce-scatter.5.cloned.1.call-update) | async-done | bytes 147472 | tf_op jit(solution)/shard_map/reduce_scatter | solution.py:41
  894.3 0.0 copy-done.1
  894.3 0.0 copy-done.3
  894.3 1.7 subtract_convert_fusion
  896.0 0.0 all-gather.8.cloned.1.call-update
  896.0 0.0 all-gather.6.cloned.1.call-start
  896.1 0.5 all-gather.6.cloned.1.call-update
  896.6 0.0 reduce-scatter.7.cloned.1.call-start
  896.7 131.6 %all-gather.8.cloned.1.call-done = bf16[4608,512]{1,0:T(8,128)(2,1)} async-done(((bf16[72,512]{1,0:T(8,128)(2,1)}), bf16[4608,512]{1,0:T(8,128)(2,1)}) %all-gather.8.cloned.1.call-update) | async-done | bytes 4718608 | tf_op jit(solution)/shard_map/all_gather | solution.py:45
  1028.3 6.6 fusion
  1034.9 6.8 copy.13
  1041.7 0.0 reduce-scatter.7.cloned.1.call-update
  1041.7 117.3 %all-gather.6.cloned.1.call-done = bf16[4608,512]{1,0:T(8,128)(2,1)} async-done(((bf16[72,512]{1,0:T(8,128)(2,1)}), bf16[4608,512]{1,0:T(8,128)(2,1)}) %all-gather.6.cloned.1.call-update) | async-done | bytes 4718608 | tf_op jit(solution)/shard_map/all_gather | solution.py:34
  1159.1 7.2 convolution_convert_fusion.1
  1166.2 48.2 %reduce-scatter.7.cloned.1.call-done = bf16[128,4608]{1,0:T(8,128)(2,1)} async-done(((bf16[512,4608]{1,0:T(8,128)(2,1)}), bf16[128,4608]{1,0:T(8,128)(2,1)}) %reduce-scatter.7.cloned.1.call-update) | async-done | bytes 1179664
  (6 shorter events, 0.0 us)
Async XLA Ops:
  7.2 60.4 %copy-start = (bf16[512,512]{1,0:T(8,128)(2,1)S(1)}, bf16[512,512]{1,0:T(8,128)(2,1)}, u32[]{:S(2)}) copy-start(bf16[512,512]{1,0:T(8,128)(2,1)} %param.7) | copy-start | bytes 1572868
  7.2 60.3 %all-gather.4.cloned.1.call-start = ((), (), s32[]{:S(2)}) async-start(), calls=%async_computation.2 | async-start | bytes 5898240 | tf_op jit(solution)/shard_map/all_gather | solution.py:28
  7.9 886.4 %reduce-scatter.5.cloned.1.call-start = ((), (), s32[]{:S(2)}) async-start(), calls=%async_computation.4 | async-start | bytes 9584640 | tf_op jit(solution)/shard_map/reduce_scatter | solution.py:41
  75.0 819.3 %copy-start.1 = (bf16[72,512]{1,0:T(8,128)(2,1)S(1)}, bf16[72,512]{1,0:T(8,128)(2,1)}, u32[]{:S(2)}) copy-start(bf16[72,512]{1,0:T(8,128)(2,1)} %param.9) | copy-start | bytes 221188
  75.0 819.3 %copy-start.2 = (f32[72,512]{1,0:T(8,128)S(1)}, f32[72,512]{1,0:T(8,128)}, u32[]{:S(2)}) copy-start(f32[72,512]{1,0:T(8,128)} %param.10) | copy-start | bytes 442372
  75.0 819.3 %copy-start.3 = (f32[72,512]{1,0:T(8,128)S(1)}, f32[72,512]{1,0:T(8,128)}, u32[]{:S(2)}) copy-start(f32[72,512]{1,0:T(8,128)} %param.11) | copy-start | bytes 442372
  75.0 953.2 %copy-start.4 = (bf16[512,512]{1,0:T(8,128)(2,1)S(1)}, bf16[512,512]{1,0:T(8,128)(2,1)}, u32[]{:S(2)}) copy-start(bf16[512,512]{1,0:T(8,128)(2,1)} %param.8) | copy-start | bytes 1572868
  75.1 953.2 %all-gather.8.cloned.1.call-start = ((), (), s32[]{:S(2)}) async-start(), calls=%async_computation.5 | async-start | bytes 4792320 | tf_op jit(solution)/shard_map/all_gather | solution.py:45
  896.0 263.0 %all-gather.6.cloned.1.call-start = ((), (), s32[]{:S(2)}) async-start(), calls=%async_computation.3 | async-start | bytes 4792320 | tf_op jit(solution)/shard_map/all_gather | solution.py:34
  896.6 317.8 %reduce-scatter.7.cloned.1.call-start = ((), (), s32[]{:S(2)}) async-start(), calls=%async_computation.6 | async-start | bytes 5898240
Sparse Core Ops, SparseCore 0:
  9.8 57.6 all-gather.3
  75.2 819.0 reduce-scatter.4
  898.5 129.6 all-gather.7
  1031.8 127.2 all-gather.5
  1162.0 52.3 reduce-scatter.6
where the time goes:
time: 1220 us
  waiting for transfers between devices  1180 us (97%)
  matrix products  21.3 us (2%)
  between operations  13.8 us (1%)
    reduce_scatter x1, waiting for transfers between devices, local(): lax.psum_scatter(product * scale, 'dp', scatter_dimension=0, tiled=True)  819 us
    all_gather x1, waiting for transfers between devices, local(): lax.all_gather(new_weight, 'dp', axis=0, tiled=True)  132 us
    all_gather x1, waiting for transfers between devices, local(): lax.all_gather(weight, 'dp', axis=0, tiled=True)  117 us
    all_gather x1, waiting for transfers between devices, local(): gathered = lax.all_gather(cotangent, 'tensor', axis=0, tiled=True)  59.6 us
    unnamed x6, waiting for transfers between devices  49.4 us
  transfers between devices with their start and end apart: 5, of which 5 were waited for; matrix products, arithmetic and copies ran while one was open for 2% of the time, Pallas kernels for 0%

commit v1 on v0

v1 whole, which is shorter than its diff:
```python
import math

import jax
import jax.numpy as jnp
from jax import lax
from jax.experimental import pallas as pl
from jax.experimental.pallas import tpu as pltpu
from jax.sharding import PartitionSpec as P

F32, BF16 = jnp.float32, jnp.bfloat16
MESH = pl.DeviceIdType.MESH

first_decay = 0.9
second_decay = 0.95
first_fix = 1.0 - 0.9**10
second_fix = 1.0 - 0.95**10
learning_rate = 0.002
weight_decay = 0.1
epsilon = 1e-08

TOKENS = 32768
OWN = 72
BLK = 2 * OWN
QR = 8 * BLK
N_COPY = 128


def nt(a, b):
    return lax.dot_general(a, b, (((1,), (1,)), ((), ())), preferred_element_type=F32)


def stack(v):
    return jnp.concatenate([v[:, :256], v[:, 256:]], axis=0).astype(BF16)


def unstack(v):
    v = v.astype(F32)
    return jnp.concatenate([v[:OWN], v[OWN:]], axis=1)


def kernel(
    c_ref, a_ref, n_ref, w_ref, m1_ref, m2_ref,
    ga_ref, nw_ref, nm1_ref, nm2_ref, out_ref,
    t32, q, ct, ab, nb, nr, g32, rs_s, rs_r, gx_s, gx_r,
    w_s, w_r, wb, wt, w2_s, w2_r, wb2, gs, gr,
    os_, ok, orv, xs, xk, xr, fy, yr,
    ssem, rsem,
):
    dp, t = lax.axis_index("dp"), lax.axis_index("tensor")
    z, xh, y = lax.div(dp, 8), lax.rem(lax.div(dp, 4), 2), lax.rem(dp, 4)
    xl, c = lax.div(t, 2), lax.rem(t, 2)

    def at(dz=0, dy=0, fxh=False, fxl=False, fc=False):
        z2, y2 = lax.rem(z + dz + 8, 8), lax.rem(y + dy + 4, 4)
        xh2 = 1 - xh if fxh else xh
        xl2 = 1 - xl if fxl else xl
        c2 = 1 - c if fc else c
        return (z2 * 8 + xh2 * 4 + y2, xl2 * 2 + c2)

    copies = []

    def send(src, dst, device):
        i = len(copies)
        copy = pltpu.make_async_remote_copy(
            src_ref=src, dst_ref=dst, send_sem=ssem.at[i], recv_sem=rsem.at[i],
            device_id=device, device_id_type=MESH,
        )
        copy.start()
        copies.append(copy)
        return copy

    def zz(d):
        return lax.rem(z + d + 8, 8)

    def yy(d):
        return lax.rem(y + d + 4, 4)

    def rows(zb, n=BLK):
        return pl.ds(pl.multiple_of(zb * n, 16), n)

    barrier = pltpu.get_barrier_semaphore()
    partners = [at(dz=1), at(dz=-1), at(dy=1), at(dy=2), at(dy=3), at(fxh=True), at(fxl=True), at(fc=True)]
    for p in partners:
        pl.semaphore_signal(barrier, inc=1, device_id=p, device_id_type=MESH)

    def turn(i, _):
        col = pl.multiple_of(i * 1152, 128)
        for j in range(9):
            t32[j * 128 : (j + 1) * 128, :] = c_ref[:, pl.ds(col + j * 128, 128)].astype(F32).T
        for b in range(2):
            for k in range(4):
                lo = b * 576 + k * OWN
                v = jnp.concatenate([t32[lo : lo + OWN, :], t32[lo + 288 : lo + 288 + OWN, :]], axis=0)
                q[k, rows(2 * i + b), :] = v.astype(BF16)
        return 0

    lax.fori_loop(0, 4, turn, 0)
    ct[y, t] = q[y]
    ab[y] = a_ref[...]
    w_s[...] = stack(w_ref[...].astype(F32))
    pl.semaphore_wait(barrier, len(partners))

    def gather_z(buf):
        sent = {}

        def hop(d, s, k):
            src = zz(-(k - 1)) if d == 0 else zz(k - 1)
            if k > 1:
                sent[d, s, k - 1].wait_recv()
            sent[d, s, k] = send(buf.at[s, rows(src)], buf.at[s, rows(src)], at(dz=1 if d == 0 else -1))

        def step(k):
            for s in range(2):
                for d in range(2):
                    if k < 4 or s == d:
                        hop(d, s, k)
                    else:
                        sent[d, s, 3].wait_recv()

        def last():
            for s in range(2):
                sent[s, s, 4].wait_recv()

        return step, last

    wx = send(w_s, w_r, at(fxh=True))
    tx = (1 - xl) * 2 + c
    x_c = {0: send(ct.at[y, t], ct.at[y, t], at(fxl=True))}
    c_c = {(0, 0): send(ct.at[y, t], ct.at[y, t], at(fc=True))}
    y_c = {}
    for d in (1, 3, 2):
        y_c[d] = send(q.at[yy(d)], ct.at[y, t], at(dy=d))
    a_c = {d: send(ab.at[y], ab.at[y], at(dy=d)) for d in (1, 3)}

    wx.wait_recv()
    mine, theirs = w_ref[...].astype(F32), unstack(w_r[...])
    both = jnp.concatenate([jnp.where(xh == 0, mine, theirs), jnp.where(xh == 0, theirs, mine)], axis=0)
    both = both.astype(BF16)
    wb[0, rows(z), :] = both[:, :256]
    wb[1, rows(z), :] = both[:, 256:]
    w_step, w_last = gather_z(wb)
    w_step(1)

    def g_block(src, zb):
        lhs = jnp.concatenate([ct[src, k, rows(zb), :] for k in range(4)], axis=1)
        return jnp.dot(lhs, ab[src], preferred_element_type=F32)

    def arrive_y(d):
        y_c[d].wait_recv()
        src = yy(-d)
        x_c[d] = send(ct.at[src, t], ct.at[src, t], at(fxl=True))
        c_c[d, 0] = send(ct.at[src, t], ct.at[src, t], at(fc=True))

    def arrive_x(d):
        x_c[d].wait_recv()
        src = yy(-d)
        c_c[d, 1] = send(ct.at[src, tx], ct.at[src, tx], at(fc=True))

    def arrive_c(d):
        c_c[d, 0].wait_recv()
        c_c[d, 1].wait_recv()

    arrive_y(1)
    arrive_y(3)
    w_step(2)
    arrive_x(0)
    arrive_c(0)

    def g_first(i, _):
        g32[rows(i), :] = g_block(y, i)
        return 0

    lax.fori_loop(0, 8, g_first, 0)
    arrive_y(2)
    w_step(3)
    arrive_x(1)
    a_c[1].wait_recv()
    a_f = {1: send(ab.at[yy(-1), pl.ds(0, 256)], ab.at[yy(-1), pl.ds(0, 256)], at(dy=1))}
    a_c[3].wait_recv()
    a_f[3] = send(ab.at[yy(1), pl.ds(256, 256)], ab.at[yy(1), pl.ds(256, 256)], at(dy=3))
    arrive_x(3)
    w_step(4)
    nb[y] = n_ref[...]
    n_c = {d: send(nb.at[y], nb.at[y], at(dy=d)) for d in (1, 3)}
    for d in (1, 3):
        arrive_c(d)

        def g_more(i, _, d=d):
            g32[rows(i), :] += g_block(yy(-d), i)
            return 0

        lax.fori_loop(0, 8, g_more, 0)
    arrive_x(2)
    arrive_c(2)
    a_f[1].wait_recv()
    a_f[3].wait_recv()

    rs = {}

    def g_end(d):
        zb = zz(d)
        g32[rows(zb), :] += g_block(yy(2), zb)

    def rs_hop(d, s, k):
        zb = zz(k if d == 0 else -k)
        acc = g32[rows(zb), s * 256 : (s + 1) * 256]
        if (d, s, k + 1) in rs:
            rs[d, s, k + 1].wait_recv()
            acc = acc + rs_r[d, s, k].astype(F32)
        rs_s[d, s, k - 1] = acc.astype(BF16)
        rs[d, s, k] = send(rs_s.at[d, s, k - 1], rs_r.at[d, s, k - 1], at(dz=1 if d == 0 else -1))

    g_end(4)
    rs_hop(0, 0, 4)
    rs_hop(1, 1, 4)
    g_end(3)
    rs_hop(0, 1, 3)
    g_end(-3)
    rs_hop(1, 0, 3)
    rs_hop(0, 0, 3)
    rs_hop(1, 1, 3)
    for k in (2, 1):
        g_end(k)
        rs_hop(0, 1, k)
        g_end(-k)
        rs_hop(1, 0, k)
        rs_hop(0, 0, k)
        rs_hop(1, 1, k)
    g_end(0)
    halves = []
    for s in range(2):
        acc = g32[rows(z), s * 256 : (s + 1) * 256]
        for d in range(2):
            rs[d, s, 1].wait_recv()
            acc = acc + rs_r[d, s, 0].astype(F32)
        halves.append(acc)
    total = jnp.concatenate(halves, axis=1)
    upper, lower = total[:OWN], total[OWN:]
    gx_s[...] = stack(jnp.where(xh == 0, lower, upper))
    gx = send(gx_s, gx_r, at(fxh=True))
    keep = jnp.where(xh == 0, upper, lower)

    n_c[1].wait_recv()
    n_f = {1: send(nb.at[yy(-1), pl.ds(0, 256)], nb.at[yy(-1), pl.ds(0, 256)], at(dy=1))}
    n_c[3].wait_recv()
    n_f[3] = send(nb.at[yy(1), pl.ds(256, 256)], nb.at[yy(1), pl.ds(256, 256)], at(dy=3))

    gx.wait_recv()
    gradient = (keep + unstack(gx_r[...])) * (1.0 / math.sqrt(TOKENS))
    new_m1 = first_decay * m1_ref[...] + (1.0 - first_decay) * gradient
    new_m2 = second_decay * m2_ref[...] + (1.0 - second_decay) * gradient * gradient
    update = new_m1 / first_fix / (jnp.sqrt(new_m2 / second_fix) + epsilon)
    new_w = w_ref[...].astype(F32) * (1.0 - learning_rate * weight_decay) - learning_rate * update
    nm1_ref[...] = new_m1
    nm2_ref[...] = new_m2
    nw_ref[...] = new_w.astype(BF16)
    w2_s[...] = stack(new_w)
    w2x = send(w2_s, w2_r, at(fxh=True))

    w_last()

    def w_turn(i, _):
        for s in range(2):
            v = wb[s, pl.ds(pl.multiple_of(i * 128, 128), 128), :].astype(F32)
            wt[s * 256 : (s + 1) * 256, pl.ds(pl.multiple_of(i * 128, 128), 128)] = v.T.astype(BF16)
        return 0

    lax.fori_loop(0, 9, w_turn, 0)

    w2x.wait_recv()
    mine, theirs = new_w, unstack(w2_r[...])
    both = jnp.concatenate([jnp.where(xh == 0, mine, theirs), jnp.where(xh == 0, theirs, mine)], axis=0)
    both = both.astype(BF16)
    wb2[0, rows(z), :] = both[:, :256]
    wb2[1, rows(z), :] = both[:, 256:]
    w2_step, w2_last = gather_z(wb2)
    w2_step(1)

    n_f[1].wait_recv()
    n_f[3].wait_recv()

    def n_turn(k, _):
        for dc in range(2):
            for dx in range(2):
                owner = (xl if dx else 1 - xl) * 2 + (c if dc else 1 - c)
                lo = pl.multiple_of(owner * 128, 128)
                to = pl.multiple_of(dx * 512 + k * 128, 128)
                nr[dc, pl.ds(to, 128), :] = nb[k, pl.ds(lo, 128), :]
        return 0

    lax.fori_loop(0, 4, n_turn, 0)

    order = (0, 1, -1, 2, -2, 3, -3, 4)
    o_c, o_x, o_y = {}, {}, []

    def out_block(i):
        zb = zz(order[i])
        lhs = jnp.concatenate([wb2[0, rows(zb), :], wb2[1, rows(zb), :]], axis=1)
        os_[zb] = nt(lhs, nr[0]).astype(BF16)
        o_c[i] = send(os_.at[zb], orv.at[zb], at(fc=True))
        ok[zb] = nt(lhs, nr[1]).astype(BF16)

    def out_core(i):
        zb = zz(order[i])
        o_c[i].wait_recv()
        v = ok[zb].astype(F32) + orv[zb].astype(F32)
        xs[zb] = v[:, :512].astype(BF16)
        o_x[i] = send(xs.at[zb], xr.at[zb], at(fxl=True))
        xk[zb] = v[:, 512:]

    def out_x(i):
        zb = zz(order[i])
        o_x[i].wait_recv()
        v = (xk[zb] + xr[zb].astype(F32)).astype(BF16)
        for k in range(4):
            fy[k, rows(zb), :] = v[:, k * 128 : (k + 1) * 128]
        for d in (1, 3, 2):
            o_y.append(send(fy.at[yy(d), rows(zb)], yr.at[y, rows(zb)], at(dy=d)))
        yr[y, rows(zb), :] = fy[y, rows(zb), :]

    def ga_part(d):
        src = yy(d)
        rhs = jnp.concatenate([ct[src, k] for k in range(4)], axis=1)
        gs[src] = jnp.dot(wt[...], rhs, preferred_element_type=F32).astype(BF16)

    ga_c = {}
    for i in range(8 + 3):
        if i in (1, 3, 5):
            w2_step(2 + (i - 1) // 2)
        if i == 7:
            w2_last()
        if i < 8:
            out_block(i)
        if 0 <= i - 1 < 8:
            out_core(i - 1)
        if i in (1, 2, 3):
            d = {1: 1, 2: 3, 3: 2}[i]
            ga_part(d)
            ga_c[d] = send(gs.at[yy(d)], gr.at[d - 1], at(dy=d))
        if 0 <= i - 3 < 8:
            out_x(i - 3)
    ga_part(0)
    acc = gs[y].astype(F32)
    for d in (1, 3, 2):
        ga_c[d].wait_recv()
        acc = acc + gr[d - 1].astype(F32)
    ga_ref[...] = acc.T.astype(BF16)

    for copy in o_y:
        copy.wait_recv()

    def back(i, _):
        for b in range(2):
            for k in range(4):
                v = yr[k, rows(2 * i + b), :].astype(F32)
                lo = b * 576 + k * OWN
                t32[lo : lo + OWN, :] = v[:OWN]
                t32[lo + 288 : lo + 288 + OWN, :] = v[OWN:]
        col = pl.multiple_of(i * 1152, 128)
        for j in range(9):
            out_ref[:, pl.ds(col + j * 128, 128)] = t32[j * 128 : (j + 1) * 128, :].T.astype(BF16)
        return 0

    lax.fori_loop(0, 4, back, 0)
    for copy in copies:
        copy.wait_send()


def local(cotangent, attn_saved, attn_next, weight, moment1, moment2):
    v = pltpu.VMEM
    scratch = [
        v((QR, 128), F32),
        v((4, QR, 128), BF16),
        v((4, 4, QR, 128), BF16),
        v((4, 512, 512), BF16),
        v((4, 512, 512), BF16),
        v((2, 1024, 512), BF16),
        v((QR, 512), F32),
        v((2, 2, 4, BLK, 256), BF16),
        v((2, 2, 4, BLK, 256), BF16),
        v((BLK, 256), BF16),
        v((BLK, 256), BF16),
        v((BLK, 256), BF16),
        v((BLK, 256), BF16),
        v((2, QR, 256), BF16),
        v((512, QR), BF16),
        v((BLK, 256), BF16),
        v((BLK, 256), BF16),
        v((2, QR, 256), BF16),
        v((4, 512, 512), BF16),
        v((3, 512, 512), BF16),
        v((8, BLK, 1024), BF16),
        v((8, BLK, 1024), BF16),
        v((8, BLK, 1024), BF16),
        v((8, BLK, 512), BF16),
        v((8, BLK, 512), F32),
        v((8, BLK, 512), BF16),
        v((4, QR, 128), BF16),
        v((4, QR, 128), BF16),
        pltpu.SemaphoreType.DMA((N_COPY,)),
        pltpu.SemaphoreType.DMA((N_COPY,)),
    ]
    vm = pl.BlockSpec(memory_space=pltpu.VMEM)
    s = jax.ShapeDtypeStruct
    return pl.pallas_call(
        kernel,
        out_shape=(
            s((512, 512), BF16),
            s((OWN, 512), BF16),
            s((OWN, 512), F32),
            s((OWN, 512), F32),
            s((128, 4608), BF16),
        ),
        in_specs=[vm] * 6,
        out_specs=(vm,) * 5,
        scratch_shapes=scratch,
        compiler_params=pltpu.CompilerParams(
            collective_id=0, has_side_effects=True, vmem_limit_bytes=60 * 2**20
        ),
        name="update",
    )(cotangent, attn_saved, attn_next, weight, moment1, moment2)


def solution(mesh):
    return jax.shard_map(
        local,
        mesh=mesh,
        in_specs=(P(("dp", "tensor"), None),) + (P("dp", "tensor"),) * 5,
        out_specs=(P("dp", "tensor"),) * 4 + (P(("dp", "tensor"), None),),
        check_vma=False,
    )
```

time: 1220 us -> 127 us (0.10)
  waiting for transfers between devices: 1180 us -> 0 us
  Pallas kernels: 0 us -> 117 us
  matrix products: 21.3 us -> 0 us
  between operations: 13.8 us -> 0.66 us
    reduce_scatter x1 -> x0, waiting for transfers between devices: 819 us -> none  [local(): lax.psum_scatter(product * scale, 'dp', scatter_dimension=0, tiled=True)]
    all_gather x3 -> x0, waiting for transfers between devices: 309 us -> none  [the longest x1 132 us: local(): lax.all_gather(new_weight, 'dp', axis=0, tiled=True)]
    pallas_call x0 -> x1, Pallas kernels: none -> 117 us  [local(): pl.pallas_call(kernel, out_shape=(s((512, 512), BF16), s((OWN, 512), BF16...]
    unnamed x6 -> x0, waiting for transfers between devices: 49.4 us -> none
    dot_general x3 -> x0, matrix products: 21.3 us -> none  [the longest x1 7.53 us: local(): lax.dot_general(columns, attn_saved, (((0,), (0,)), ((), ())), preferred_...]
  transfers between devices with their start and end apart: 5 -> 0, of which waited for: 5 -> 0; matrix products, arithmetic and copies ran while one was open for 2% -> 0% of each run, Pallas kernels for 0% -> 0%
where the time goes in v1:
time: 127 us; the launch traced here: 125 us
  Pallas kernels  117 us (92%)
  local copies, waits for them, and re-layouts  6.75 us (5%)
    pallas_call x1, Pallas kernels, local(): pl.pallas_call(kernel, out_shape=(s((512, 512), BF16), s((OWN, 512), BF16...  117 us
    unnamed x9, local copies, waits for them, and re-layouts  6.75 us

profile of v1, /device:TPU:1, one launch (start us, length us, event | category | flops | bytes accessed | tf_op | source)
XLA Modules:
  0.0 124.7 jit_solution(17646134627025895541)
XLA Ops:
  0.6 117.3 %update.1 = (bf16[512,512]{1,0:T(8,128)(2,1)}, bf16[72,512]{1,0:T(8,128)(2,1)}, f32[72,512]{1,0:T(8,128)}, f32[72,512]{1,0:T(8,128)}, bf16[128,4608]{1,0:T(8,128)(2,1)}) custom-call(bf16[128,4608]{1,0:T(8,128)(2,1)} %c_ref.1, bf16[512,512]{1,0:T(8,128)(2,1)} %a_ref.1, bf16[512,512]{1,0:T(8,128)(2,1)} %n_ref.1, bf16[72,512]{1,0:T(8,128)(2,1)} %w_ref.1, ...), custom_call_target="tpu_custom_call" | custom-call | tf_op jit(solution)/shard_map/update/pallas_call | solution.py:405
  118.0 0.0 copy-start.1
  118.0 0.0 copy-start
  118.0 2.0 %copy.16 = bf16[512,512]{1,0:T(8,128)(2,1)} copy(bf16[512,512]{1,0:T(8,128)(2,1)} %get-tuple-element.10) | data formatting | bytes 1048576
  119.9 1.5 %copy.17 = bf16[72,512]{1,0:T(8,128)(2,1)} copy(bf16[72,512]{1,0:T(8,128)(2,1)} %get-tuple-element.11) | data formatting | bytes 147456
  121.5 1.6 %copy.18 = f32[72,512]{1,0:T(8,128)} copy(f32[72,512]{1,0:T(8,128)} %get-tuple-element.12) | data formatting | bytes 294912
  123.0 0.0 copy-done.1
  123.0 0.7 copy.19
  123.7 0.0 copy-done
  123.7 1.0 copy.20
Async XLA Ops:
  118.0 5.1 %copy-start.1 = (f32[72,512]{1,0:T(8,128)S(1)}, f32[72,512]{1,0:T(8,128)}, u32[]{:S(2)}) copy-start(f32[72,512]{1,0:T(8,128)} %get-tuple-element.13) | copy-start | bytes 442372
  118.0 5.7 %copy-start = (bf16[128,4608]{1,0:T(8,128)(2,1)S(1)}, bf16[128,4608]{1,0:T(8,128)(2,1)}, u32[]{:S(2)}) copy-start(bf16[128,4608]{1,0:T(8,128)(2,1)} %get-tuple-element.14) | copy-start | bytes 3538948

commit v2 on v1

--- a/solution.py
+++ b/solution.py
@@ -39,12 +39,12 @@
 
 
 def kernel(
-    c_ref, a_ref, n_ref, w_ref, m1_ref, m2_ref,
+    c_hbm, a_hbm, n_hbm, w_hbm, m1_hbm, m2_hbm,
     ga_ref, nw_ref, nm1_ref, nm2_ref, out_ref,
-    t32, q, ct, ab, nb, nr, g32, rs_s, rs_r, gx_s, gx_r,
+    c_ref, w_ref, m1_ref, m2_ref, t32, q, ct, ab, nb, nr, g32, rs_s, rs_r, gx_s, gx_r,
     w_s, w_r, wb, wt, w2_s, w2_r, wb2, gs, gr,
     os_, ok, orv, xs, xk, xr, fy, yr,
-    ssem, rsem,
+    ssem, rsem, lsem,
 ):
     dp, t = lax.axis_index("dp"), lax.axis_index("tensor")
     z, xh, y = lax.div(dp, 8), lax.rem(lax.div(dp, 4), 2), lax.rem(dp, 4)
@@ -78,6 +78,14 @@
     def rows(zb, n=BLK):
         return pl.ds(pl.multiple_of(zb * n, 16), n)
 
+    loads = [
+        pltpu.make_async_copy(src, dst, lsem.at[i])
+        for i, (src, dst) in enumerate(
+            ((c_hbm, c_ref), (w_hbm, w_ref), (a_hbm, ab.at[y]), (n_hbm, nb.at[y]), (m1_hbm, m1_ref), (m2_hbm, m2_ref))
+        )
+    ]
+    for load in loads:
+        load.start()
     barrier = pltpu.get_barrier_semaphore()
     partners = [at(dz=1), at(dz=-1), at(dy=1), at(dy=2), at(dy=3), at(fxh=True), at(fxl=True), at(fc=True)]
     for p in partners:
@@ -94,9 +102,10 @@
                 q[k, rows(2 * i + b), :] = v.astype(BF16)
         return 0
 
+    loads[0].wait()
     lax.fori_loop(0, 4, turn, 0)
     ct[y, t] = q[y]
-    ab[y] = a_ref[...]
+    loads[1].wait()
     w_s[...] = stack(w_ref[...].astype(F32))
     pl.semaphore_wait(barrier, len(partners))
 
@@ -123,21 +132,71 @@
 
         return step, last
 
+    tx = (1 - xl) * 2 + c
+    x_c, c_c, y_c = {}, {}, {}
+
+    def c_on(d):
+        src = yy(-d)
+        if d:
+            y_c[d].wait_recv()
+        x_c[d] = send(ct.at[src, t], ct.at[src, t], at(fxl=True))
+        c_c[d, 0] = send(ct.at[src, t], ct.at[src, t], at(fc=True))
+
+    def c_y(d):
+        y_c[d] = send(q.at[yy(d)], ct.at[y, t], at(dy=d))
+
+    def c_core(d):
+        x_c[d].wait_recv()
+        src = yy(-d)
+        c_c[d, 1] = send(ct.at[src, tx], ct.at[src, tx], at(fc=True))
+
+    def c_all(d):
+        c_c[d, 0].wait_recv()
+        c_c[d, 1].wait_recv()
+
+    def over_y(buf):
+        first, rest, then = {}, {}, {}
+        low = {1: 0, 3: 256}
+
+        def one():
+            for d in (1, 3):
+                part = buf.at[y, pl.ds(low[d], 256)]
+                first[d] = send(part, part, at(dy=d))
+
+        def one_more():
+            for d in (1, 3):
+                part = buf.at[y, pl.ds(256 - low[d], 256)]
+                rest[d] = send(part, part, at(dy=d))
+
+        def two():
+            for d in (1, 3):
+                first[d].wait_recv()
+                part = buf.at[yy(-d), pl.ds(low[d], 256)]
+                then[d] = send(part, part, at(dy=d))
+
+        def last():
+            for d in (1, 3):
+                rest[d].wait_recv()
+                then[d].wait_recv()
+
+        return one, one_more, two, last
+
+    a_one, a_more, a_two, a_last = over_y(ab)
+    n_one, n_more, n_two, n_last = over_y(nb)
+
+    c_y(1)
+    c_y(3)
+    c_on(0)
     wx = send(w_s, w_r, at(fxh=True))
-    tx = (1 - xl) * 2 + c
-    x_c = {0: send(ct.at[y, t], ct.at[y, t], at(fxl=True))}
-    c_c = {(0, 0): send(ct.at[y, t], ct.at[y, t], at(fc=True))}
-    y_c = {}
-    for d in (1, 3, 2):
-        y_c[d] = send(q.at[yy(d)], ct.at[y, t], at(dy=d))
-    a_c = {d: send(ab.at[y], ab.at[y], at(dy=d)) for d in (1, 3)}
+
+    def both_x(mine, theirs):
+        v = jnp.concatenate([jnp.where(xh == 0, mine, theirs), jnp.where(xh == 0, theirs, mine)], axis=0)
+        return v.astype(BF16)
 
     wx.wait_recv()
-    mine, theirs = w_ref[...].astype(F32), unstack(w_r[...])
-    both = jnp.concatenate([jnp.where(xh == 0, mine, theirs), jnp.where(xh == 0, theirs, mine)], axis=0)
-    both = both.astype(BF16)
-    wb[0, rows(z), :] = both[:, :256]
-    wb[1, rows(z), :] = both[:, 256:]
+    v = both_x(w_ref[...].astype(F32), unstack(w_r[...]))
+    wb[0, rows(z), :] = v[:, :256]
+    wb[1, rows(z), :] = v[:, 256:]
     w_step, w_last = gather_z(wb)
     w_step(1)
 
@@ -145,57 +204,49 @@
         lhs = jnp.concatenate([ct[src, k, rows(zb), :] for k in range(4)], axis=1)
         return jnp.dot(lhs, ab[src], preferred_element_type=F32)
 
-    def arrive_y(d):
-        y_c[d].wait_recv()
-        src = yy(-d)
-        x_c[d] = send(ct.at[src, t], ct.at[src, t], at(fxl=True))
-        c_c[d, 0] = send(ct.at[src, t], ct.at[src, t], at(fc=True))
-
-    def arrive_x(d):
-        x_c[d].wait_recv()
-        src = yy(-d)
-        c_c[d, 1] = send(ct.at[src, tx], ct.at[src, tx], at(fc=True))
-
-    def arrive_c(d):
-        c_c[d, 0].wait_recv()
-        c_c[d, 1].wait_recv()
-
-    arrive_y(1)
-    arrive_y(3)
+    def g_part(d):
+        def body(i, _):
+            v = g_block(yy(-d), i)
+            g32[rows(i), :] = v if d == 0 else g32[rows(i), :] + v
+            return 0
+
+        lax.fori_loop(0, 8, body, 0)
+
+    c_on(1)
+    c_on(3)
+    c_y(2)
     w_step(2)
-    arrive_x(0)
-    arrive_c(0)
-
-    def g_first(i, _):
-        g32[rows(i), :] = g_block(y, i)
+    c_core(0)
+    c_all(0)
+    loads[2].wait()
+    a_one()
+    g_part(0)
+    c_on(2)
+    a_more()
+    w_step(3)
+    a_two()
+    c_core(1)
+    c_core(3)
+    w_step(4)
+
+    def w_turn(i, _):
+        for s in range(2):
+            v = wb[s, pl.ds(pl.multiple_of(i * 128, 128), 128), :].astype(F32)
+            wt[s * 256 : (s + 1) * 256, pl.ds(pl.multiple_of(i * 128, 128), 128)] = v.T.astype(BF16)
         return 0
 
-    lax.fori_loop(0, 8, g_first, 0)
-    arrive_y(2)
-    w_step(3)
-    arrive_x(1)
-    a_c[1].wait_recv()
-    a_f = {1: send(ab.at[yy(-1), pl.ds(0, 256)], ab.at[yy(-1), pl.ds(0, 256)], at(dy=1))}
-    a_c[3].wait_recv()
-    a_f[3] = send(ab.at[yy(1), pl.ds(256, 256)], ab.at[yy(1), pl.ds(256, 256)], at(dy=3))
-    arrive_x(3)
-    w_step(4)
-    nb[y] = n_ref[...]
-    n_c = {d: send(nb.at[y], nb.at[y], at(dy=d)) for d in (1, 3)}
-    for d in (1, 3):
-        arrive_c(d)
-
-        def g_more(i, _, d=d):
-            g32[rows(i), :] += g_block(yy(-d), i)
-            return 0
-
-        lax.fori_loop(0, 8, g_more, 0)
-    arrive_x(2)
-    arrive_c(2)
-    a_f[1].wait_recv()
-    a_f[3].wait_recv()
-
-    rs = {}
+    c_all(1)
+    a_last()
+    loads[3].wait()
+    n_one()
+    g_part(1)
+    c_core(2)
+    c_all(3)
+    g_part(3)
+    c_all(2)
+    n_more()
+
+    rs, ga_c = {}, {}
 
     def g_end(d):
         zb = zz(d)
@@ -210,6 +261,14 @@
         rs_s[d, s, k - 1] = acc.astype(BF16)
         rs[d, s, k] = send(rs_s.at[d, s, k - 1], rs_r.at[d, s, k - 1], at(dz=1 if d == 0 else -1))
 
+    def ga_part(d):
+        src = yy(d)
+        rhs = jnp.concatenate([ct[src, k] for k in range(4)], axis=1)
+        gs[src] = jnp.dot(wt[...], rhs, preferred_element_type=F32).astype(BF16)
+
+    def ga_send(d):
+        ga_c[d] = send(gs.at[yy(d)], gr.at[d - 1], at(dy=d))
+
     g_end(4)
     rs_hop(0, 0, 4)
     rs_hop(1, 1, 4)
@@ -217,16 +276,25 @@
     rs_hop(0, 1, 3)
     g_end(-3)
     rs_hop(1, 0, 3)
+    g_end(2)
+    g_end(-2)
+    w_last()
+    lax.fori_loop(0, 9, w_turn, 0)
     rs_hop(0, 0, 3)
     rs_hop(1, 1, 3)
     for k in (2, 1):
-        g_end(k)
+        if k == 1:
+            ga_part(3)
         rs_hop(0, 1, k)
-        g_end(-k)
         rs_hop(1, 0, k)
+        if k == 2:
+            g_end(1)
+            g_end(-1)
+            g_end(0)
+            ga_part(1)
         rs_hop(0, 0, k)
         rs_hop(1, 1, k)
-    g_end(0)
+    ga_part(2)
     halves = []
     for s in range(2):
         acc = g32[rows(z), s * 256 : (s + 1) * 256]
@@ -240,44 +308,27 @@
     gx = send(gx_s, gx_r, at(fxh=True))
     keep = jnp.where(xh == 0, upper, lower)
 
-    n_c[1].wait_recv()
-    n_f = {1: send(nb.at[yy(-1), pl.ds(0, 256)], nb.at[yy(-1), pl.ds(0, 256)], at(dy=1))}
-    n_c[3].wait_recv()
-    n_f[3] = send(nb.at[yy(1), pl.ds(256, 256)], nb.at[yy(1), pl.ds(256, 256)], at(dy=3))
+    n_two()
+    ga_send(1)
+    ga_send(3)
+    ga_part(0)
 
     gx.wait_recv()
+    loads[4].wait()
+    loads[5].wait()
     gradient = (keep + unstack(gx_r[...])) * (1.0 / math.sqrt(TOKENS))
     new_m1 = first_decay * m1_ref[...] + (1.0 - first_decay) * gradient
     new_m2 = second_decay * m2_ref[...] + (1.0 - second_decay) * gradient * gradient
     update = new_m1 / first_fix / (jnp.sqrt(new_m2 / second_fix) + epsilon)
     new_w = w_ref[...].astype(F32) * (1.0 - learning_rate * weight_decay) - learning_rate * update
+    w2_s[...] = stack(new_w)
+    w2x = send(w2_s, w2_r, at(fxh=True))
     nm1_ref[...] = new_m1
     nm2_ref[...] = new_m2
     nw_ref[...] = new_w.astype(BF16)
-    w2_s[...] = stack(new_w)
-    w2x = send(w2_s, w2_r, at(fxh=True))
-
-    w_last()
-
-    def w_turn(i, _):
-        for s in range(2):
-            v = wb[s, pl.ds(pl.multiple_of(i * 128, 128), 128), :].astype(F32)
-            wt[s * 256 : (s + 1) * 256, pl.ds(pl.multiple_of(i * 128, 128), 128)] = v.T.astype(BF16)
-        return 0
-
-    lax.fori_loop(0, 9, w_turn, 0)
-
-    w2x.wait_recv()
-    mine, theirs = new_w, unstack(w2_r[...])
-    both = jnp.concatenate([jnp.where(xh == 0, mine, theirs), jnp.where(xh == 0, theirs, mine)], axis=0)
-    both = both.astype(BF16)
-    wb2[0, rows(z), :] = both[:, :256]
-    wb2[1, rows(z), :] = both[:, 256:]
-    w2_step, w2_last = gather_z(wb2)
-    w2_step(1)
-
-    n_f[1].wait_recv()
-    n_f[3].wait_recv()
+
+    n_last()
+    ga_send(2)
 
     def n_turn(k, _):
         for dc in range(2):
@@ -289,6 +340,13 @@
         return 0
 
     lax.fori_loop(0, 4, n_turn, 0)
+
+    w2x.wait_recv()
+    v = both_x(new_w, unstack(w2_r[...]))
+    wb2[0, rows(z), :] = v[:, :256]
+    wb2[1, rows(z), :] = v[:, 256:]
+    w2_step, w2_last = gather_z(wb2)
+    w2_step(1)
 
     order = (0, 1, -1, 2, -2, 3, -3, 4)
     o_c, o_x, o_y = {}, {}, []
@@ -318,12 +376,6 @@
             o_y.append(send(fy.at[yy(d), rows(zb)], yr.at[y, rows(zb)], at(dy=d)))
         yr[y, rows(zb), :] = fy[y, rows(zb), :]
 
-    def ga_part(d):
-        src = yy(d)
-        rhs = jnp.concatenate([ct[src, k] for k in range(4)], axis=1)
-        gs[src] = jnp.dot(wt[...], rhs, preferred_element_type=F32).astype(BF16)
-
-    ga_c = {}
     for i in range(8 + 3):
         if i in (1, 3, 5):
             w2_step(2 + (i - 1) // 2)
@@ -333,13 +385,8 @@
             out_block(i)
         if 0 <= i - 1 < 8:
             out_core(i - 1)
-        if i in (1, 2, 3):
-            d = {1: 1, 2: 3, 3: 2}[i]
-            ga_part(d)
-            ga_c[d] = send(gs.at[yy(d)], gr.at[d - 1], at(dy=d))
         if 0 <= i - 3 < 8:
             out_x(i - 3)
-    ga_part(0)
     acc = gs[y].astype(F32)
     for d in (1, 3, 2):
         ga_c[d].wait_recv()
@@ -366,9 +413,21 @@
         copy.wait_send()
 
 
+def put(*refs):
+    copies = [pltpu.make_async_copy(refs[i], refs[5 + i], refs[10].at[i]) for i in range(5)]
+    for copy in copies:
+        copy.start()
+    for copy in copies:
+        copy.wait()
+
+
 def local(cotangent, attn_saved, attn_next, weight, moment1, moment2):
     v = pltpu.VMEM
     scratch = [
+        v((128, 4608), BF16),
+        v((OWN, 512), BF16),
+        v((OWN, 512), F32),
+        v((OWN, 512), F32),
         v((QR, 128), F32),
         v((4, QR, 128), BF16),
         v((4, 4, QR, 128), BF16),
@@ -399,26 +458,37 @@
         v((4, QR, 128), BF16),
         pltpu.SemaphoreType.DMA((N_COPY,)),
         pltpu.SemaphoreType.DMA((N_COPY,)),
+        pltpu.SemaphoreType.DMA((6,)),
     ]
     vm = pl.BlockSpec(memory_space=pltpu.VMEM)
     s = jax.ShapeDtypeStruct
-    return pl.pallas_call(
+    shapes = (
+        s((512, 512), BF16),
+        s((OWN, 512), BF16),
+        s((OWN, 512), F32),
+        s((OWN, 512), F32),
+        s((128, 4608), BF16),
+    )
+    results = pl.pallas_call(
         kernel,
-        out_shape=(
-            s((512, 512), BF16),
-            s((OWN, 512), BF16),
-            s((OWN, 512), F32),
-            s((OWN, 512), F32),
-            s((128, 4608), BF16),
-        ),
-        in_specs=[vm] * 6,
+        out_shape=tuple(v(x.shape, x.dtype) for x in shapes),
+        in_specs=[pl.BlockSpec(memory_space=pltpu.HBM)] * 6,
         out_specs=(vm,) * 5,
         scratch_shapes=scratch,
         compiler_params=pltpu.CompilerParams(
-            collective_id=0, has_side_effects=True, vmem_limit_bytes=60 * 2**20
+            collective_id=0, has_side_effects=True, vmem_limit_bytes=64 * 2**20 - 2150000
         ),
         name="update",
     )(cotangent, attn_saved, attn_next, weight, moment1, moment2)
+    return pl.pallas_call(
+        put,
+        out_shape=shapes,
+        in_specs=[vm] * 5,
+        out_specs=(pl.BlockSpec(memory_space=pl.ANY),) * 5,
+        scratch_shapes=[pltpu.SemaphoreType.DMA((5,))],
+        compiler_params=pltpu.CompilerParams(vmem_limit_bytes=4 * 2**20),
+        name="put",
+    )(*results)
 
 
 def solution(mesh):

time: 127 us -> 114 us (0.90); the launches traced: 125 us -> 114 us
  local copies, waits for them, and re-layouts: 6.75 us -> 0 us
  Pallas kernels: 117 us -> 113 us
    unnamed x9 -> x0, local copies, waits for them, and re-layouts: 6.75 us -> none
    pallas_call x1 -> x2, Pallas kernels: 117 us -> 113 us  [the longest x1 112 us: local(): pl.pallas_call(kernel, out_shape=tuple((v(x.shape, x.dtype) for x in shap...]
where the time goes in v2:
time: 114 us
  Pallas kernels  113 us (99%)
    pallas_call x1, Pallas kernels, local(): pl.pallas_call(kernel, out_shape=tuple((v(x.shape, x.dtype) for x in shap...  112 us

profile of v2, /device:TPU:1, one launch (start us, length us, event | category | flops | bytes accessed | tf_op | source)
XLA Modules:
  0.0 114.0 jit_solution(12943452975261319327)
XLA Ops:
  0.6 112.0 %update.1 = (bf16[512,512]{1,0:T(8,128)(2,1)S(1)}, bf16[72,512]{1,0:T(8,128)(2,1)S(1)}, f32[72,512]{1,0:T(8,128)S(1)}, f32[72,512]{1,0:T(8,128)S(1)}, bf16[128,4608]{1,0:T(8,128)(2,1)S(1)}) custom-call(bf16[128,4608]{1,0:T(8,128)(2,1)} %c_hbm.1, bf16[512,512]{1,0:T(8,128)(2,1)} %a_hbm.1, bf16[512,512]{1,0:T(8,128)(2,1)} %n_hbm.1, bf16[72,512]{1,0:T(8,128)(2,1)} %w_hbm.1, ...), custom_call_target="tpu_custom_call" | custom-call | tf_op jit(solution)/shard_map/update/pallas_call | solution.py:472
  112.7 1.4 %put.1 = (bf16[512,512]{1,0:T(8,128)(2,1)}, bf16[72,512]{1,0:T(8,128)(2,1)}, f32[72,512]{1,0:T(8,128)}, f32[72,512]{1,0:T(8,128)}, bf16[128,4608]{1,0:T(8,128)(2,1)}) custom-call(bf16[512,512]{1,0:T(8,128)(2,1)S(1)} %get-tuple-element.10.refs_0_, bf16[72,512]{1,0:T(8,128)(2,1)S(1)} %get-tuple-element.11.refs_1_, f32[72,512]{1,0:T(8,128)S(1)} %get-tuple-element.12.refs_2_, ...), custom_call_target="tpu_custom_call" | custom-call | tf_op jit(solution)/shard_map/put/pallas_call | solution.py:483

commit v3 on v2

--- a/solution.py
+++ b/solution.py
@@ -184,9 +184,9 @@
     a_one, a_more, a_two, a_last = over_y(ab)
     n_one, n_more, n_two, n_last = over_y(nb)
 
+    c_on(0)
     c_y(1)
     c_y(3)
-    c_on(0)
     wx = send(w_s, w_r, at(fxh=True))
 
     def both_x(mine, theirs):
@@ -292,6 +292,7 @@
             g_end(-1)
             g_end(0)
             ga_part(1)
+            n_two()
         rs_hop(0, 0, k)
         rs_hop(1, 1, k)
     ga_part(2)
@@ -308,7 +309,6 @@
     gx = send(gx_s, gx_r, at(fxh=True))
     keep = jnp.where(xh == 0, upper, lower)
 
-    n_two()
     ga_send(1)
     ga_send(3)
     ga_part(0)
@@ -351,12 +351,16 @@
     order = (0, 1, -1, 2, -2, 3, -3, 4)
     o_c, o_x, o_y = {}, {}, []
 
-    def out_block(i):
-        zb = zz(order[i])
-        lhs = jnp.concatenate([wb2[0, rows(zb), :], wb2[1, rows(zb), :]], axis=1)
-        os_[zb] = nt(lhs, nr[0]).astype(BF16)
-        o_c[i] = send(os_.at[zb], orv.at[zb], at(fc=True))
-        ok[zb] = nt(lhs, nr[1]).astype(BF16)
+    def out_block(ids):
+        zs = [zz(order[i]) for i in ids]
+        lhs = [jnp.concatenate([wb2[0, rows(zb), :], wb2[1, rows(zb), :]], axis=1) for zb in zs]
+        lhs = lhs[0] if len(lhs) == 1 else jnp.concatenate(lhs, axis=0)
+        for dc, to in ((0, os_), (1, ok)):
+            v = nt(lhs, nr[dc]).astype(BF16)
+            for j, i in enumerate(ids):
+                to[zs[j]] = v[j * BLK : (j + 1) * BLK]
+                if dc == 0:
+                    o_c[i] = send(os_.at[zs[j]], orv.at[zs[j]], at(fc=True))
 
     def out_core(i):
         zb = zz(order[i])
@@ -382,7 +386,10 @@
         if i == 7:
             w2_last()
         if i < 8:
-            out_block(i)
+            if i in (0, 7):
+                out_block((i,))
+            elif i % 2:
+                out_block((i, i + 1))
         if 0 <= i - 1 < 8:
             out_core(i - 1)
         if 0 <= i - 3 < 8:

time: 114 us -> 114 us (level)
  no operation moved by 1% of the time
where the time goes in v3:
time: 114 us
  Pallas kernels  113 us (99%)
    pallas_call x1, Pallas kernels, local(): pl.pallas_call(kernel, out_shape=tuple((v(x.shape, x.dtype) for x in shap...  112 us

profile of v3, /device:TPU:1, one launch (start us, length us, event | category | flops | bytes accessed | tf_op | source)
XLA Modules:
  0.0 114.0 jit_solution(925274443109995619)
XLA Ops:
  0.6 112.0 %update.1 = (bf16[512,512]{1,0:T(8,128)(2,1)S(1)}, bf16[72,512]{1,0:T(8,128)(2,1)S(1)}, f32[72,512]{1,0:T(8,128)S(1)}, f32[72,512]{1,0:T(8,128)S(1)}, bf16[128,4608]{1,0:T(8,128)(2,1)S(1)}) custom-call(bf16[128,4608]{1,0:T(8,128)(2,1)} %c_hbm.1, bf16[512,512]{1,0:T(8,128)(2,1)} %a_hbm.1, bf16[512,512]{1,0:T(8,128)(2,1)} %n_hbm.1, bf16[72,512]{1,0:T(8,128)(2,1)} %w_hbm.1, ...), custom_call_target="tpu_custom_call" | custom-call | tf_op jit(solution)/shard_map/update/pallas_call | solution.py:479
  112.6 1.4 %put.1 = (bf16[512,512]{1,0:T(8,128)(2,1)}, bf16[72,512]{1,0:T(8,128)(2,1)}, f32[72,512]{1,0:T(8,128)}, f32[72,512]{1,0:T(8,128)}, bf16[128,4608]{1,0:T(8,128)(2,1)}) custom-call(bf16[512,512]{1,0:T(8,128)(2,1)S(1)} %get-tuple-element.10.refs_0_, bf16[72,512]{1,0:T(8,128)(2,1)S(1)} %get-tuple-element.11.refs_1_, f32[72,512]{1,0:T(8,128)S(1)} %get-tuple-element.12.refs_2_, ...), custom_call_target="tpu_custom_call" | custom-call | tf_op jit(solution)/shard_map/put/pallas_call | solution.py:490
